TPU v7x, 32 devices: a whole 2x2x4 slice. The times are simulated.
32 devices in a mesh: ctx: 8 (over z, y), tp: 4 (over x, core).
Axes of the slice: x: 2, y: 2, z: 4, core: 2. Of those that a mesh axis runs over, the one named last changes fastest.
Arguments:
- queries: bfloat16 [2048, 8192], P('ctx', 'tp'), may hold values from -6 to 6
- new_keys: bfloat16 [2048, 1024], P('ctx', 'tp'), may hold values from -6 to 6
- new_values: bfloat16 [2048, 1024], P('ctx', 'tp'), may hold values from -6 to 6
- positions: int32 [2048], P('ctx'), may hold values from 0 to 262143, as said below
- cache_keys: bfloat16 [16384, 1024], P('ctx', 'tp'), may hold values from -6 to 6
- cache_values: bfloat16 [16384, 1024], P('ctx', 'tp'), may hold values from -6 to 6
- pattern: int32 [32, 4], P('ctx'), may hold values from 0 to 7, all different within a row; in each aligned block of 4 rows (0 to 3, 4 to 7, ...) at most 2 rows name the same one
- out_weight: bfloat16 [8192, 8192], P('tp'), may hold values from -0.0625 to 0.0625
Outputs:
- mixed: bfloat16 [2048, 8192], P(('ctx', 'tp'))
Inputs may be any that keep to these rules, and one draw needn't show every extreme that they name: All 2048 positions are distinct. `pattern`: each row names 4 different segments; among the 4 query blocks of one ctx device at most 2 name the same segment, and 2 do in some devices.
All inputs are finite; a program needn't handle non-finite values.
Results may differ from a plain program's by a relative error of at most 0.0075.
Values may be sent and summed in bfloat16 or wider, within the bound.
A program may use at most 128 MiB of HBM per device.

v0:
```python
import math

import jax
import jax.numpy as jnp
from jax import lax
from jax.sharding import PartitionSpec as P

H = 64
KVH = 8
HD = 128
TOPB = 4
CAP = 2


NEG_FILL = -1e30


def local_partial(query_heads, key_rows, value_rows, scaling):
    scores = (
        jnp.einsum("tgrd,sgd->tgrs", query_heads, key_rows, preferred_element_type=jnp.float32)
        * scaling
    )
    largest = jnp.max(scores, axis=-1)
    weights = jnp.exp(scores - largest[..., None])
    totals = jnp.sum(weights, axis=-1)
    mixed_values = jnp.einsum(
        "tgrs,sgd->tgrd",
        weights.astype(jnp.bfloat16),
        value_rows,
        preferred_element_type=jnp.float32,
    )
    return (mixed_values / totals[..., None], largest + jnp.log(totals))


def absorb(running, part_log, part_out):
    run_max, run_sum, run_out = running
    gated_log = jnp.where(True, part_log, NEG_FILL)
    new_max = jnp.maximum(run_max, gated_log)
    decay_old = jnp.exp(run_max - new_max)
    weight_new = jnp.where(True, jnp.exp(gated_log - new_max), 0.0)
    return (
        new_max,
        run_sum * decay_old + weight_new,
        run_out * decay_old[..., None] + weight_new[..., None] * part_out,
    )


def per_device(
    queries, new_keys, new_values, positions, cache_keys, cache_values, pattern, out_weight
):
    ctx_count = lax.axis_size("ctx")
    group_size = H // KVH
    scaling = 1.0 / math.sqrt(HD)
    token_count = queries.shape[0]
    feature_width = queries.shape[1]
    head_count = feature_width // HD
    kv_count = cache_keys.shape[1] // HD
    block_count = pattern.shape[0]
    rows_per_block = token_count // block_count
    query_heads = queries.reshape(token_count, kv_count, group_size, HD)
    resident_keys = cache_keys.reshape(cache_keys.shape[0], kv_count, HD)
    resident_values = cache_values.reshape(cache_values.shape[0], kv_count, HD)
    start_state = (
        jnp.full((token_count, kv_count, group_size), NEG_FILL, jnp.float32),
        jnp.zeros((token_count, kv_count, group_size), jnp.float32),
        jnp.zeros((token_count, kv_count, group_size, HD), jnp.float32),
    )
    fresh_keys = new_keys.reshape(token_count, kv_count, HD)
    fresh_values = new_values.reshape(token_count, kv_count, HD)
    running = start_state
    key_part = lax.all_gather(fresh_keys, "ctx", axis=0, tiled=True)
    value_part = lax.all_gather(fresh_values, "ctx", axis=0, tiled=True)
    position_part = lax.all_gather(positions, "ctx", axis=0, tiled=True)
    shards = key_part.shape[0] // token_count

    def one_shard(folded, shard_data):
        shard_keys, shard_values, shard_positions = shard_data
        run_max, run_sum, run_acc = folded
        scores = (
            jnp.einsum(
                "tgrd,sgd->tgrs", query_heads, shard_keys, preferred_element_type=jnp.float32
            )
            * scaling
        )
        visible = (shard_positions[None, :] <= positions[:, None])[:, None, None, :]
        masked = jnp.where(visible, scores, NEG_FILL)
        new_max = jnp.maximum(run_max, jnp.max(masked, axis=-1))
        weights = jnp.where(visible, jnp.exp(masked - new_max[..., None]), 0.0)
        decay_old = jnp.exp(run_max - new_max)
        run_acc = run_acc * decay_old[..., None] + jnp.einsum(
            "tgrs,sgd->tgrd",
            weights.astype(jnp.bfloat16),
            shard_values,
            preferred_element_type=jnp.float32,
        )
        return ((new_max, run_sum * decay_old + jnp.sum(weights, axis=-1), run_acc), None)

    stacked = (
        key_part.reshape(shards, token_count, kv_count, HD),
        value_part.reshape(shards, token_count, kv_count, HD),
        position_part.reshape(shards, token_count),
    )
    running, unused = lax.scan(one_shard, running, stacked)
    fresh_max, fresh_sum, fresh_acc = running
    fresh_out = (fresh_acc / fresh_sum[..., None]).reshape(token_count, head_count, HD)
    fresh_log = (fresh_max + jnp.log(fresh_sum)).reshape(token_count, head_count)
    running = (fresh_log, jnp.ones_like(fresh_log), fresh_out)
    flat_targets = pattern.reshape(-1)
    entry_count = flat_targets.shape[0]
    slot_total = ctx_count * CAP
    target_hits = (flat_targets[:, None] == jnp.arange(ctx_count, dtype=jnp.int32)[None, :]).astype(
        jnp.int32
    )
    earlier = jnp.cumsum(target_hits, axis=0) - target_hits
    slot_ranks = jnp.sum(earlier * target_hits, axis=1)
    slot_of_entry = flat_targets * CAP + slot_ranks
    owners = (slot_of_entry[None, :] == jnp.arange(slot_total, dtype=jnp.int32)[:, None]).astype(
        jnp.int32
    )
    source_block = jnp.sum(
        owners * (jnp.arange(entry_count, dtype=jnp.int32) // TOPB)[None, :], axis=1
    )
    query_blocks = queries.reshape(block_count, rows_per_block, feature_width)
    outgoing = jnp.take(query_blocks, source_block, axis=0).reshape(
        ctx_count, CAP, rows_per_block, feature_width
    )
    incoming = lax.all_to_all(outgoing, "ctx", split_axis=0, concat_axis=0, tiled=True)

    def one_source(slot_queries):
        slot_count = slot_queries.shape[0]
        heads_view = slot_queries.reshape(slot_count * rows_per_block, kv_count, group_size, HD)
        part_out, part_log = local_partial(heads_view, resident_keys, resident_values, scaling)
        return (
            part_out.reshape(slot_count, rows_per_block, feature_width),
            part_log.reshape(slot_count, rows_per_block, head_count),
        )

    part_out, part_log = lax.map(one_source, incoming)
    returned_out, returned_log = (
        lax.all_to_all(part_out, "ctx", split_axis=0, concat_axis=0, tiled=True),
        lax.all_to_all(part_log, "ctx", split_axis=0, concat_axis=0, tiled=True),
    )
    picked_out = jnp.take(
        returned_out.reshape(slot_total, rows_per_block, feature_width), slot_of_entry, axis=0
    )
    picked_out = picked_out.reshape(block_count, TOPB, rows_per_block, head_count, HD)
    picked_log = jnp.take(
        returned_log.reshape(slot_total, rows_per_block, head_count), slot_of_entry, axis=0
    )
    picked_log = picked_log.reshape(block_count, TOPB, rows_per_block, head_count)
    for column in range(TOPB):
        running = absorb(
            running,
            picked_log[:, column].reshape(token_count, head_count),
            picked_out[:, column].reshape(token_count, head_count, HD),
        )
    run_max, run_sum, run_out = running
    attention = (
        (run_out / run_sum[..., None]).reshape(token_count, feature_width).astype(jnp.bfloat16)
    )
    return lax.psum_scatter(
        jnp.dot(attention, out_weight, preferred_element_type=jnp.float32),
        "tp",
        scatter_dimension=0,
        tiled=True,
    ).astype(jnp.bfloat16)


def solution(mesh):
    placed = (
        P("ctx", "tp"),
        P("ctx", "tp"),
        P("ctx", "tp"),
        P("ctx"),
        P("ctx", "tp"),
        P("ctx", "tp"),
        P("ctx", None),
        P("tp", None),
    )
    return jax.shard_map(
        per_device, mesh=mesh, in_specs=placed, out_specs=P(("ctx", "tp"), None), check_vma=False
    )
```

profile of v0, /device:TPU:0, one launch (start us, length us, event | category | flops | bytes accessed | tf_op | source)
XLA Modules:
  0.0 635.9 jit_solution(11520605299543733943)
XLA Ops:
  7.8 4.0 gather_fusion
  11.8 4.6 broadcast_select_fusion.1
  16.5 7.4 %all-to-all-start = ((bf16[8,2,64,2048]{3,2,1,0:T(8,128)(2,1)}), bf16[8,2,64,2048]{3,2,1,0:T(8,128)(2,1)}, u32[]{:S(2)}, u32[]{:S(2)}) async-start(bf16[8,2,64,2048]{3,2,1,0:T(8,128)(2,1)} %broadcast_select_fusion.1), calls=%async_computation | async-start | bytes 8388608 | tf_op jit(solution)/shard_map/all_to_all | solution.py:127
  30.3 99.6 %all-to-all-done = bf16[8,2,64,2048]{3,2,1,0:T(8,128)(2,1)} async-done(((bf16[8,2,64,2048]{3,2,1,0:T(8,128)(2,1)}), bf16[8,2,64,2048]{3,2,1,0:T(8,128)(2,1)}, u32[]{:S(2)}, u32[]{:S(2)}) %all-to-all-start) | async-done | bytes 4194336 | tf_op jit(solution)/shard_map/all_to_all | solution.py:127
  129.9 106.4 %while.27 = (s32[]{:T(128)}, f32[8,2,64,2048]{3,2,1,0:T(8,128)}, f32[8,2,64,16]{2,3,1,0:T(8,128)S(1)}, bf16[8,2,64,2048]{3,2,1,0:T(8,128)(2,1)}, bf16[2048,2,128...) while((s32[]{:T(128)}, f32[8,2,64,2048]{3,2,1,0:T(8,128)}, ...), condition=%wide.region_10.11_spmd, body=%wide.region_7.10_spmd.sunk | while | flops 2181298176 | bytes 70893720 | solution.py:138
  133.9 3.3 fusion.72
  137.2 3.5 fusion.73
  144.8 2.4 bitcast_reduce_fusion.2
  147.2 3.3 fusion.72
  150.5 3.5 fusion.73
  158.1 2.4 bitcast_reduce_fusion.2
  160.5 3.3 fusion.72
  163.8 3.5 fusion.73
  171.3 2.4 bitcast_reduce_fusion.2
  173.8 3.3 fusion.72
  177.1 3.5 fusion.73
  184.6 2.4 bitcast_reduce_fusion.2
  187.1 3.3 fusion.72
  190.4 3.5 fusion.73
  197.9 2.4 bitcast_reduce_fusion.2
  200.3 3.3 fusion.72
  203.6 3.5 fusion.73
  211.2 2.4 bitcast_reduce_fusion.2
  213.6 3.3 fusion.72
  216.9 3.5 fusion.73
  224.5 2.4 bitcast_reduce_fusion.2
  226.9 3.3 fusion.72
  230.2 3.5 fusion.73
  237.0 3.5 all-to-all-start.1
  240.5 21.0 %all-gather = s32[8,1,256]{2,1,0:T(1,128)S(1)} all-gather(s32[1,1,256]{2,1,0:T(1,128)S(1)} %bitcast.267), channel_id=1, replica_groups=mesh['ctx'=8,'tp'=4] {'ctx'}, dimensions={0}, use_global_device_ids=true | all-gather | bytes 9216 | tf_op jit(solution)/shard_map/all_gather | solution.py:73
  267.0 4.9 all-to-all-start.2
  272.3 51.3 %while.28 = (s32[]{:T(128)}, f32[256,2,8]{0,2,1:T(8,128)S(1)}, f32[256,2,8]{0,2,1:T(8,128)S(1)}, f32[256,2,8,128]{0,3,2,1:T(8,128)}, s32[8,256]{1,0:T(8,128)S(1)...) while((s32[]{:T(128)}, f32[256,2,8]{0,2,1:T(8,128)S(1)}, ...), condition=%wide.region_3.4_spmd.clone, body=%wide.region_0.3_spmd.clone.sunk | while | flops 552161280 | bytes 35393732 | solution.py:103
  274.8 2.6 bitcast_add_fusion.3
  281.2 2.6 bitcast_add_fusion.3
  287.6 2.6 bitcast_add_fusion.3
  294.0 2.6 bitcast_add_fusion.3
  300.4 2.6 bitcast_add_fusion.3
  306.8 2.6 bitcast_add_fusion.3
  313.2 2.6 bitcast_add_fusion.3
  319.6 2.6 bitcast_add_fusion.3
  323.5 3.1 broadcast_divide_fusion
  332.1 119.1 %all-to-all-done.2 = f32[8,2,64,2048]{3,2,1,0:T(8,128)} async-done(((f32[8,2,64,2048]{3,2,1,0:T(8,128)}), f32[8,2,64,2048]{3,2,1,0:T(8,128)}, u32[]{:S(2)}, u32[]{:S(2)}) %all-to-all-start.2) | async-done | bytes 8388640 | tf_op jit(solution)/shard_map/all_to_all | solution.py:140
  451.2 7.7 %gather_fusion.2 = f32[16,64,2048]{2,1,0:T(8,128)} fusion(f32[16,64,2048]{2,1,0:T(8,128)} %bitcast.24, s32[1024]{0:T(1024)S(1)} %pad_clamp_fusion), kind=kCustom, calls=%fused_computation.2 | custom fusion | bytes 16777280 | tf_op jit(solution)/shard_map/jit(_take)/gather | solution.py:143
  458.9 5.4 copy.140
  465.2 3.4 fusion.56
  486.1 69.6 %fusion.44 = f32[256,8192]{1,0:T(8,128)} fusion(bf16[2048,8192]{1,0:T(8,128)(2,1)} %param.19, f32[32,8,16,128]{3,2,1,0:T(8,128)} %bitcast.250, f32[32,8,16,128]{3,2,1,0:T(8,128)} %bitcast.253, f32[32,8,16,128]{3,2,1,0:T(8,128)} %bitcast.242, f32[32,8,16,128]{3,2,1,0:T(8,128)} %bitcast.243, f32[32,8,16,128]{3,2,1,0:T(8,128)} %bitcast.254, ...), kind=kOutput, calls=%fused_computation.65 | convolution fusion | flops 8597274624 | bytes 71303168 | tf_op jit(solution)/shard_map/dot_general | solution.py:162
  555.7 70.9 %reduce-scatter.2.cloned.1.call-done = f32[64,8192]{1,0:T(8,128)} async-done(((f32[256,8192]{1,0:T(8,128)}), f32[64,8192]{1,0:T(8,128)}) %reduce-scatter.2.cloned.1.call-update) | async-done | bytes 2097168 | tf_op jit(solution)/shard_map/reduce_scatter | solution.py:161
  626.5 2.7 convert_element_type.18
  (277 shorter events, 102.6 us)
Async XLA Ops:
  16.5 7.5 %copy-start.7 = (bf16[256,256]{1,0:T(8,128)(2,1)S(1)}, bf16[256,256]{1,0:T(8,128)(2,1)}, u32[]{:S(2)}) copy-start(bf16[256,256]{1,0:T(8,128)(2,1)} %param.13) | copy-start | bytes 393220
  16.5 8.3 %copy-start.8 = (bf16[256,256]{1,0:T(8,128)(2,1)S(1)}, bf16[256,256]{1,0:T(8,128)(2,1)}, u32[]{:S(2)}) copy-start(bf16[256,256]{1,0:T(8,128)(2,1)} %param.14) | copy-start | bytes 393220
  16.5 9.2 %copy-start = (bf16[256,2048]{1,0:T(8,128)(2,1)S(1)}, bf16[256,2048]{1,0:T(8,128)(2,1)}, u32[]{:S(2)}) copy-start(bf16[256,2048]{1,0:T(8,128)(2,1)} %param.12) | copy-start | bytes 3145732
  16.5 113.4 %all-to-all-start = ((bf16[8,2,64,2048]{3,2,1,0:T(8,128)(2,1)}), bf16[8,2,64,2048]{3,2,1,0:T(8,128)(2,1)}, u32[]{:S(2)}, u32[]{:S(2)}) async-start(bf16[8,2,64,2048]{3,2,1,0:T(8,128)(2,1)} %broadcast_select_fusion.1), calls=%async_computation | async-start | bytes 8388608 | tf_op jit(solution)/shard_map/all_to_all | solution.py:127
  23.9 3.1 copy-start.10
  23.9 3.2 copy-start.3
  23.9 239.2 %all-gather.4.cloned.1.call-start = ((), (), s32[]{:S(2)}) async-start(), calls=%async_computation.4 | async-start | bytes 1179648 | tf_op jit(solution)/shard_map/all_gather | solution.py:71
  24.7 240.0 %all-gather.6.cloned.1.call-start = ((), (), s32[]{:S(2)}) async-start(), calls=%async_computation.5 | async-start | bytes 1179648 | tf_op jit(solution)/shard_map/all_gather | solution.py:72
  27.7 1.2 copy-start.4
  129.9 110.6 %copy-start.9 = (s32[256]{0:T(256)S(1)}, s32[256]{0:T(256)}, u32[]{:S(2)}) copy-start(s32[256]{0:T(256)} %param.15) | copy-start | bytes 3076
  129.9 7.3 %copy-start.5 = (bf16[2048,2,128]{2,0,1:T(8,128)(2,1)}, bf16[2048,2,128]{2,0,1:T(8,128)(2,1)S(1)}, u32[]{:S(2)}) copy-start(bf16[2048,2,128]{2,0,1:T(8,128)(2,1)S(1)} %get-tuple-element.362) | copy-start | bytes 3145732 | tf_op jit(solution)/shard_map/while
  141.6 1.6 copy-start.6
  143.2 7.3 %copy-start.5 = (bf16[2048,2,128]{2,0,1:T(8,128)(2,1)}, bf16[2048,2,128]{2,0,1:T(8,128)(2,1)S(1)}, u32[]{:S(2)}) copy-start(bf16[2048,2,128]{2,0,1:T(8,128)(2,1)S(1)} %get-tuple-element.362) | copy-start | bytes 3145732 | tf_op jit(solution)/shard_map/while
  154.9 1.6 copy-start.6
  156.5 7.3 %copy-start.5 = (bf16[2048,2,128]{2,0,1:T(8,128)(2,1)}, bf16[2048,2,128]{2,0,1:T(8,128)(2,1)S(1)}, u32[]{:S(2)}) copy-start(bf16[2048,2,128]{2,0,1:T(8,128)(2,1)S(1)} %get-tuple-element.362) | copy-start | bytes 3145732 | tf_op jit(solution)/shard_map/while
  168.2 1.6 copy-start.6
  169.8 7.3 %copy-start.5 = (bf16[2048,2,128]{2,0,1:T(8,128)(2,1)}, bf16[2048,2,128]{2,0,1:T(8,128)(2,1)S(1)}, u32[]{:S(2)}) copy-start(bf16[2048,2,128]{2,0,1:T(8,128)(2,1)S(1)} %get-tuple-element.362) | copy-start | bytes 3145732 | tf_op jit(solution)/shard_map/while
  181.5 1.6 copy-start.6
  183.1 7.3 %copy-start.5 = (bf16[2048,2,128]{2,0,1:T(8,128)(2,1)}, bf16[2048,2,128]{2,0,1:T(8,128)(2,1)S(1)}, u32[]{:S(2)}) copy-start(bf16[2048,2,128]{2,0,1:T(8,128)(2,1)S(1)} %get-tuple-element.362) | copy-start | bytes 3145732 | tf_op jit(solution)/shard_map/while
  194.8 1.6 copy-start.6
  196.4 7.3 %copy-start.5 = (bf16[2048,2,128]{2,0,1:T(8,128)(2,1)}, bf16[2048,2,128]{2,0,1:T(8,128)(2,1)S(1)}, u32[]{:S(2)}) copy-start(bf16[2048,2,128]{2,0,1:T(8,128)(2,1)S(1)} %get-tuple-element.362) | copy-start | bytes 3145732 | tf_op jit(solution)/shard_map/while
  208.0 1.6 copy-start.6
  209.7 7.3 %copy-start.5 = (bf16[2048,2,128]{2,0,1:T(8,128)(2,1)}, bf16[2048,2,128]{2,0,1:T(8,128)(2,1)S(1)}, u32[]{:S(2)}) copy-start(bf16[2048,2,128]{2,0,1:T(8,128)(2,1)S(1)} %get-tuple-element.362) | copy-start | bytes 3145732 | tf_op jit(solution)/shard_map/while
  221.3 1.6 copy-start.6
  222.9 7.3 %copy-start.5 = (bf16[2048,2,128]{2,0,1:T(8,128)(2,1)}, bf16[2048,2,128]{2,0,1:T(8,128)(2,1)S(1)}, u32[]{:S(2)}) copy-start(bf16[2048,2,128]{2,0,1:T(8,128)(2,1)S(1)} %get-tuple-element.362) | copy-start | bytes 3145732 | tf_op jit(solution)/shard_map/while
  234.6 1.6 copy-start.6
  237.0 30.1 %all-to-all-start.1 = ((f32[8,1,2048]{2,1,0:T(1,128)}), f32[8,1,2048]{2,1,0:T(1,128)S(1)}, u32[]{:S(2)}, u32[]{:S(2)}) async-start(f32[8,1,2048]{2,1,0:T(1,128)} %reshape.403), calls=%async_computation.1 | async-start | bytes 131072 | tf_op jit(solution)/shard_map/all_to_all | solution.py:141
  267.0 184.1 %all-to-all-start.2 = ((f32[8,2,64,2048]{3,2,1,0:T(8,128)}), f32[8,2,64,2048]{3,2,1,0:T(8,128)}, u32[]{:S(2)}, u32[]{:S(2)}) async-start(f32[8,2,64,2048]{3,2,1,0:T(8,128)} %get-tuple-element.91), calls=%async_computation.2 | async-start | bytes 16777216 | tf_op jit(solution)/shard_map/all_to_all | solution.py:140
  272.0 354.6 %reduce-scatter.2.cloned.1.call-start = ((), (), s32[]{:S(2)}) async-start(), calls=%async_computation.6 | async-start | bytes 10485760 | tf_op jit(solution)/shard_map/reduce_scatter | solution.py:161
  273.2 1.6 copy-start.1
  277.4 1.3 copy-start.2
  279.6 1.6 copy-start.1
  283.8 1.3 copy-start.2
  286.0 1.6 copy-start.1
  290.2 1.3 copy-start.2
  292.4 1.6 copy-start.1
  296.6 1.3 copy-start.2
  298.8 1.6 copy-start.1
  303.0 1.3 copy-start.2
  305.2 1.6 copy-start.1
  309.4 1.3 copy-start.2
  311.6 1.6 copy-start.1
  315.8 1.3 copy-start.2
  318.0 1.6 copy-start.1
  322.2 1.3 copy-start.2
Sparse Core Ops, SparseCore 0:
  26.8 87.3 all-gather.3
  116.2 41.8 all-gather.5
  555.8 70.7 reduce-scatter.1
where the time goes:
time: 639 us; the launch traced here: 636 us
  waiting for transfers between devices  290 us (45%)
  matrix products  144 us (23%)
  local copies, waits for them, and re-layouts  103 us (16%)
  other arithmetic  48.2 us (8%)
  blocking collectives  21 us (3%)
  starting transfers between devices  16.2 us (3%)
  between operations  13.6 us (2%)
    all_to_all x1, waiting for transfers between devices, per_device(): lax.all_to_all(part_out, 'ctx', split_axis=0, concat_axis=0, tiled=True)  119 us
    all_to_all x1, waiting for transfers between devices, per_device(): lax.all_to_all(outgoing, 'ctx', split_axis=0, concat_axis=0, tiled=True)  99.6 us
    reduce_scatter x1, waiting for transfers between devices, per_device(): lax.psum_scatter(jnp.dot(attention, out_weight, preferred_element_type=jn...  70.9 us
    dot_general x1, matrix products, per_device(): jnp.dot(attention, out_weight, preferred_element_type=jnp.float32)  69.6 us
    dot_general x8, matrix products, local_partial(): jnp.einsum('tgrs,sgd->tgrd', weights.astype(jnp.bfloat16), value_rows, pr...  28.1 us
    reduce_sum x8, other arithmetic, local_partial(): totals = jnp.sum(weights, axis=-1)  26.3 us
    all_gather x1, blocking collectives, per_device(): position_part = lax.all_gather(positions, 'ctx', axis=0, tiled=True)  21 us
    dot_general x8, matrix products, one_shard(): jnp.einsum('tgrs,sgd->tgrd', weights.astype(jnp.bfloat16), shard_values,...  20.5 us
  transfers between devices with their start and end apart: 6, of which 3 were waited for; matrix products, arithmetic and copies ran while one was open for 25% of the time, Pallas kernels for 0%

commit v1 on v0

v1 whole, which is shorter than its diff:
```python
import functools
import math

import jax
import jax.numpy as jnp
from jax import lax
from jax.experimental import pallas as pl
from jax.experimental.pallas import tpu as pltpu
from jax.sharding import PartitionSpec as P

H = 64
KVH = 8
HD = 128
TOPB = 4
CAP = 2
ROWS = 256
NEG_FILL = -1e30
LOG2E = math.log2(math.e)
SCALE2 = LOG2E / math.sqrt(HD)


def nt_dot(a, b):
    return lax.dot_general(a, b, (((1,), (1,)), ((), ())), preferred_element_type=jnp.float32)


def attention_kernel(
    n, q_ref, k_ref, v_ref, fresh_ref, meta_ref, column_ref, slot_ref, out_ref,
    q_all, meta_all, fr_all, kk, vv, fk, fv, bias, qsel, o_out, o_in, l_out, l_in, fo, fl,
    local_sem, kv_send, kv_recv, q_send, q_recv, m_send, m_recv, f_send, f_recv,
    mp_send, fp_send, o_send, o_recv, l_send, l_recv,
):
    planes = n // 2
    tokens = q_ref.shape[0]
    heads = q_ref.shape[1] // HD
    groups = k_ref.shape[1] // HD
    per_group = heads // groups
    block = tokens // 4
    me = lax.axis_index("ctx")
    par = lax.rem(me, 2)
    here = lax.div(me, 2)
    mate = me + 1 - 2 * par

    def column(plane):
        return {"ctx": 2 * plane + par}

    barrier = pltpu.get_barrier_semaphore()
    for step in range(1, planes):
        pl.semaphore_signal(
            barrier, inc=1, device_id=column(lax.rem(here + step, planes)),
            device_id_type=pl.DeviceIdType.MESH,
        )
    pl.semaphore_signal(
        barrier, inc=1, device_id={"ctx": mate}, device_id_type=pl.DeviceIdType.MESH
    )
    pl.semaphore_wait(barrier, planes)

    def remote(src, dst, send, recv, target):
        return pltpu.make_async_remote_copy(
            src_ref=src, dst_ref=dst, send_sem=send, recv_sem=recv, device_id=target,
            device_id_type=pl.DeviceIdType.MESH,
        )

    def chain(kind, s, side):
        target = column(s if side is None else here + 1 if side else here - 1)
        side = side or 0
        if kind == "q":
            return remote(q_all.at[s], q_all.at[s], q_send.at[side, s], q_recv.at[s], target)
        g = 2 * s + par
        if kind == "m":
            return remote(meta_all.at[g], meta_all.at[g], m_send.at[side, s], m_recv.at[g], target)
        return remote(fr_all.at[g], fr_all.at[g], f_send.at[side, s], f_recv.at[g], target)

    def to_mate(kind, s):
        g = 2 * s + par
        if kind == "m":
            return remote(meta_all.at[g], meta_all.at[g], mp_send.at[s], m_recv.at[g], {"ctx": mate})
        return remote(fr_all.at[g], fr_all.at[g], fp_send.at[s], f_recv.at[g], {"ctx": mate})

    def on_sides(s, act):
        @pl.when(jnp.logical_and(s <= here, here + 1 < planes))
        def _():
            act(1)

        @pl.when(jnp.logical_and(s >= here, here >= 1))
        def _():
            act(0)

    locals_ = [
        pltpu.make_async_copy(meta_ref, meta_all.at[me], local_sem.at[0]),
        pltpu.make_async_copy(q_ref, q_all.at[here], local_sem.at[1]),
        pltpu.make_async_copy(fresh_ref, fr_all.at[me], local_sem.at[2]),
    ]
    kv_copies = []
    for g in range(groups):
        cols = pl.ds(g * HD, HD)
        locals_.append(
            pltpu.make_async_copy(k_ref.at[:, cols], kk.at[par, g], local_sem.at[3 + 2 * g])
        )
        locals_.append(
            pltpu.make_async_copy(
                v_ref.at[:, cols], vv.at[par, g, :, pl.ds(0, HD)], local_sem.at[4 + 2 * g]
            )
        )
        kv_copies.append(
            remote(k_ref.at[:, cols], kk.at[par, g], kv_send.at[2 * g], kv_recv.at[2 * g],
                   {"ctx": mate})
        )
        kv_copies.append(
            remote(v_ref.at[:, cols], vv.at[par, g, :, pl.ds(0, HD)], kv_send.at[2 * g + 1],
                   kv_recv.at[2 * g + 1], {"ctx": mate})
        )
    for c in locals_:
        c.start()
    for c in locals_[:3]:
        c.wait()
    for kind in ("m", "q", "f"):
        on_sides(here, lambda side, kind=kind: chain(kind, here, side).start())
    to_mate("m", here).start()
    to_mate("f", here).start()
    for c in kv_copies:
        c.start()
    ones = jnp.ones((vv.shape[2], HD), jnp.bfloat16)
    for e in range(2):
        for g in range(groups):
            vv[e, g, :, HD:] = ones
    for c in locals_[3:]:
        c.wait()

    def soft(scores):
        top = jnp.max(scores, axis=1, keepdims=True)
        return top, jnp.exp2(scores - top).astype(jnp.bfloat16)

    def choose(s, e):
        g = 2 * s + par
        for r in range(CAP):
            row = (2 * here + e) * CAP + r
            which = meta_all[g, pl.ds(row, 1), :][:, :HD]
            marks = [jnp.broadcast_to(which, (block, HD)) == b for b in range(3)]
            for h in range(heads):
                cut = [
                    q_all[s, b * block:(b + 1) * block, h * HD:(h + 1) * HD].astype(jnp.float32)
                    for b in range(4)
                ]
                got = jnp.where(
                    marks[0], cut[0],
                    jnp.where(marks[1], cut[1], jnp.where(marks[2], cut[2], cut[3])),
                )
                qsel[h, r * block:(r + 1) * block, :] = got.astype(jnp.bfloat16)

    def work(s, e, outs, logs):
        choose(s, e)
        span = 2 * block

        def step(i, carry):
            g = lax.div(i, per_group // 2)
            q = qsel[pl.ds(2 * i, 2)].reshape(2 * span, HD)
            scores = nt_dot(q, kk[e, g]) * SCALE2
            top, weights = soft(scores)
            both = jnp.dot(weights, vv[e, g], preferred_element_type=jnp.float32)
            total = both[:, HD:]
            result = both[:, :HD] / total
            log = top + jnp.log2(total)
            for j in range(2):
                h = 2 * i + j
                lanes = pl.ds(pl.multiple_of(h * HD, HD), HD)
                for r in range(CAP):
                    a = j * span + r * block
                    outs[s, e, r, :, lanes] = result[a:a + block].astype(jnp.bfloat16)
                    logs[s, e, r, pl.ds(h, 1), pl.ds(0, block)] = log[a:a + block].T[:1]
            return carry

        lax.fori_loop(0, heads // 2, step, 0)

    def returns(s, e):
        return (
            remote(o_out.at[s, e], o_in.at[here, e], o_send.at[s, e], o_recv.at[here, e], column(s)),
            remote(l_out.at[s, e], l_in.at[here, e], l_send.at[s, e], l_recv.at[here, e], column(s)),
        )

    def others(act):
        def at_distance(k, carry):
            @pl.when(here - k >= 0)
            def _():
                act(here - k)

            @pl.when(here + k < planes)
            def _():
                act(here + k)

            return carry

        lax.fori_loop(1, planes, at_distance, 0)

    work(here, par, o_in, l_in)

    def first_half(s):
        for kind in ("m", "q", "f"):
            chain(kind, s, None).wait_recv()
            on_sides(s, lambda side, kind=kind: chain(kind, s, side).start())
            if kind != "q":
                to_mate(kind, s).start()
        work(s, par, o_out, l_out)
        for c in returns(s, par):
            c.start()

    others(first_half)
    for c in kv_copies:
        c.wait()

    def second_half(s):
        work(s, 1 - par, o_out, l_out)
        for c in returns(s, 1 - par):
            c.start()

    others(second_half)
    work(here, 1 - par, o_in, l_in)

    def from_mate(s, carry):
        g = 2 * s + 1 - par
        remote(meta_all.at[g], meta_all.at[g], mp_send.at[s], m_recv.at[g], {"ctx": mate}).wait_recv()
        remote(fr_all.at[g], fr_all.at[g], fp_send.at[s], f_recv.at[g], {"ctx": mate}).wait_recv()
        return carry

    lax.fori_loop(0, planes, from_mate, 0)
    mine = jnp.broadcast_to(column_ref[...], (tokens, tokens))
    for d in range(n):
        there = jnp.broadcast_to(meta_all[d, 2 * n:2 * n + 1, :], (tokens, tokens))
        bias[:, d * tokens:(d + 1) * tokens] = jnp.where(there <= mine, 0.0, NEG_FILL)
        for g in range(groups):
            rows = slice(d * tokens, (d + 1) * tokens)
            fk[g, rows, :] = fr_all[d, 0, :, g * HD:(g + 1) * HD]
            fv[g, rows, :HD] = fr_all[d, 1, :, g * HD:(g + 1) * HD]
    for g in range(groups):
        fv[g, :, HD:] = jnp.ones((n * tokens, HD), jnp.bfloat16)

    def fresh_head(h, carry):
        g = lax.div(h, per_group)
        lanes = pl.ds(pl.multiple_of(h * HD, HD), HD)
        scores = nt_dot(q_ref[:, lanes], fk[g]) * SCALE2 + bias[...]
        top, weights = soft(scores)
        both = jnp.dot(weights, fv[g], preferred_element_type=jnp.float32)
        total = both[:, HD:]
        fo[:, lanes] = both[:, :HD] / total
        fl[h] = top + jnp.log2(total)
        return carry

    lax.fori_loop(0, heads, fresh_head, 0)

    def arrived(s):
        for e in range(2):
            remote(o_out.at[s, e], o_in.at[s, e], o_send.at[s, e], o_recv.at[s, e], column(s)).wait_recv()
            remote(l_out.at[s, e], l_in.at[s, e], l_send.at[s, e], l_recv.at[s, e], column(s)).wait_recv()

    others(arrived)
    for b in range(4):
        rows = slice(b * block, (b + 1) * block)
        slots = [slot_ref[b * TOPB + j] for j in range(TOPB)]
        spots = [
            (lax.div(x, 4), lax.rem(lax.div(x, 2), 2), lax.rem(x, 2)) for x in slots
        ]
        tables = [l_in[p, e, r].T for p, e, r in spots]
        for h in range(heads):
            logs = [
                jnp.broadcast_to(t[:block, h:h + 1], (block, HD)) for t in tables
            ] + [fl[h, rows, :]]
            top = functools.reduce(jnp.maximum, logs)
            shares = [jnp.exp2(x - top) for x in logs]
            whole = functools.reduce(jnp.add, shares)
            lanes = slice(h * HD, (h + 1) * HD)
            mixed = shares[-1] * fo[rows, lanes]
            for (p, e, r), w in zip(spots, shares):
                mixed = mixed + w * o_in[p, e, r, :, lanes].astype(jnp.float32)
            out_ref[rows, lanes] = (mixed / whole).astype(out_ref.dtype)

    def sent(s, carry):
        on_sides(s, lambda side: [chain(kind, s, side).wait_send() for kind in ("m", "q", "f")])
        to_mate("m", s).wait_send()
        to_mate("f", s).wait_send()
        return carry

    lax.fori_loop(0, planes, sent, 0)

    def back(s):
        for e in range(2):
            for c in returns(s, e):
                c.wait_send()

    others(back)


def attend(n, queries, keys, values, fresh, meta, column, slots):
    planes = n // 2
    tokens, width = queries.shape
    heads = width // HD
    groups = keys.shape[1] // HD
    span = keys.shape[0]
    block = tokens // 4
    vmem = pl.BlockSpec(memory_space=pltpu.VMEM)
    bf, f32 = jnp.bfloat16, jnp.float32
    dma = pltpu.SemaphoreType.DMA
    return pl.pallas_call(
        functools.partial(attention_kernel, n),
        out_shape=jax.ShapeDtypeStruct((tokens, width), bf),
        in_specs=[vmem] * 6 + [pl.BlockSpec(memory_space=pltpu.SMEM)],
        out_specs=vmem,
        scratch_shapes=[
            pltpu.VMEM((planes, tokens, width), bf),
            pltpu.VMEM((n,) + meta.shape, jnp.int32),
            pltpu.VMEM((n,) + fresh.shape, bf),
            pltpu.VMEM((2, groups, span, HD), bf),
            pltpu.VMEM((2, groups, span, 2 * HD), bf),
            pltpu.VMEM((groups, n * tokens, HD), bf),
            pltpu.VMEM((groups, n * tokens, 2 * HD), bf),
            pltpu.VMEM((tokens, n * tokens), f32),
            pltpu.VMEM((heads, 2 * block, HD), bf),
            pltpu.VMEM((planes, 2, CAP, block, width), bf),
            pltpu.VMEM((planes, 2, CAP, block, width), bf),
            pltpu.VMEM((planes, 2, CAP, heads, HD), f32),
            pltpu.VMEM((planes, 2, CAP, heads, HD), f32),
            pltpu.VMEM((tokens, width), f32),
            pltpu.VMEM((heads, tokens, HD), f32),
            dma((3 + 2 * groups,)),
            dma((2 * groups,)),
            dma((2 * groups,)),
            dma((2, planes)),
            dma((planes,)),
            dma((2, planes)),
            dma((n,)),
            dma((2, planes)),
            dma((n,)),
            dma((planes,)),
            dma((planes,)),
            dma((planes, 2)),
            dma((planes, 2)),
            dma((planes, 2)),
            dma((planes, 2)),
        ],
        compiler_params=pltpu.CompilerParams(
            collective_id=0, has_side_effects=True, vmem_limit_bytes=62 * 1024 * 1024
        ),
    )(queries, keys, values, fresh, meta, column, slots)


def per_device(
    queries, new_keys, new_values, positions, cache_keys, cache_values, pattern, out_weight
):
    n = lax.axis_size("ctx")
    tokens = queries.shape[0]
    flat = pattern.reshape(-1)
    hits = (flat[:, None] == jnp.arange(n, dtype=jnp.int32)[None, :]).astype(jnp.int32)
    earlier = jnp.cumsum(hits, axis=0) - hits
    slots = flat * CAP + jnp.sum(earlier * hits, axis=1)
    owners = (slots[None, :] == jnp.arange(n * CAP, dtype=jnp.int32)[:, None]).astype(jnp.int32)
    blocks = jnp.sum(owners * (jnp.arange(flat.shape[0], dtype=jnp.int32) // TOPB)[None, :], axis=1)
    meta = jnp.concatenate(
        [
            jnp.broadcast_to(blocks[:, None], (n * CAP, tokens)),
            jnp.broadcast_to(positions[None, :], (8, tokens)),
        ],
        axis=0,
    )
    fresh = jnp.stack([new_keys, new_values])
    attention = attend(
        n, queries, cache_keys, cache_values, fresh, meta, positions.reshape(tokens, 1), slots
    )
    part = jnp.dot(attention, out_weight, preferred_element_type=jnp.float32).astype(jnp.bfloat16)
    return lax.psum_scatter(part, "tp", scatter_dimension=0, tiled=True)


def solution(mesh):
    placed = (
        P("ctx", "tp"),
        P("ctx", "tp"),
        P("ctx", "tp"),
        P("ctx"),
        P("ctx", "tp"),
        P("ctx", "tp"),
        P("ctx", None),
        P("tp", None),
    )
    return jax.shard_map(
        per_device, mesh=mesh, in_specs=placed, out_specs=P(("ctx", "tp"), None), check_vma=False
    )
```

time: 639 us -> 344 us (0.54)
  Pallas kernels: 0 us -> 265 us
  waiting for transfers between devices: 290 us -> 42.9 us
  matrix products: 144 us -> 16.7 us
  local copies, waits for them, and re-layouts: 103 us -> 2.91 us
  other arithmetic: 48.2 us -> 2.78 us
  blocking collectives: 21 us -> 0 us
  starting transfers between devices: 16.2 us -> 0.01 us
    pallas_call x0 -> x1, Pallas kernels: none -> 265 us  [attend(): pl.pallas_call(functools.partial(attention_kernel, n), out_shape=jax.Shap...]
    all_to_all x3 -> x0, waiting for transfers between devices: 219 us -> none  [the longest x1 119 us: per_device(): lax.all_to_all(part_out, 'ctx', split_axis=0, concat_axis=0, tiled=True)]
    dot_general x32 -> x0, matrix products: 74 us -> none  [the longest x8 28.1 us: local_partial(): jnp.einsum('tgrs,sgd->tgrd', weights.astype(jnp.bfloat16), value_rows, pr...]
    dot_general x1, matrix products: 69.6 us -> 16.7 us  [per_device(): jnp.dot(attention, out_weight, preferred_element_type=jnp.float32)]
    reduce_sum x18 -> x2, other arithmetic: 34.7 us -> 0.3 us  [the longest x1 0.19 us: per_device(): slots = flat * CAP + jnp.sum(earlier * hits, axis=1)]
    reduce_scatter x1, waiting for transfers between devices: 70.9 us -> 42.9 us  [per_device(): return lax.psum_scatter(part, 'tp', scatter_dimension=0, tiled=True)]
    while x82 -> x0, local copies, waits for them, and re-layouts: 21.3 us -> none
    all_gather x1 -> x0, blocking collectives: 21 us -> none  [per_device(): position_part = lax.all_gather(positions, 'ctx', axis=0, tiled=True)]
  transfers between devices with their start and end apart: 6 -> 1, of which waited for: 3 -> 1; matrix products, arithmetic and copies ran while one was open for 25% -> 0% of each run, Pallas kernels for 0% -> 0%
where the time goes in v1:
time: 344 us; the launch traced here: 343 us
  Pallas kernels  265 us (77%)
  waiting for transfers between devices  42.9 us (12%)
  matrix products  16.7 us (5%)
  between operations  13.4 us (4%)
    pallas_call x1, Pallas kernels, attend(): pl.pallas_call(functools.partial(attention_kernel, n), out_shape=jax.Shap...  265 us
    reduce_scatter x1, waiting for transfers between devices, per_device(): return lax.psum_scatter(part, 'tp', scatter_dimension=0, tiled=True)  42.9 us
    dot_general x1, matrix products, per_device(): jnp.dot(attention, out_weight, preferred_element_type=jnp.float32)  16.7 us
  transfers between devices with their start and end apart: 1, of which 1 were waited for; matrix products, arithmetic and copies ran while one was open for 0% of the time, Pallas kernels for 0%

profile of v1, /device:TPU:0, one launch (start us, length us, event | category | flops | bytes accessed | tf_op | source)
XLA Modules:
  0.0 343.3 jit_solution(12043145786426934402)
XLA Ops:
  6.5 0.0 reduce-scatter.2.cloned.1.call-start
  6.5 0.8 reshape.30
  7.3 0.1 fusion
  7.4 0.2 select_reduce_fusion.1
  7.6 0.0 copy-start
  7.6 0.1 select_reduce_fusion
  7.7 1.5 copy.10.column_ref
  9.2 0.7 broadcast_in_dim.5
  9.9 0.7 pad_add_fusion.meta_ref
  10.5 1.7 pad_maximum_fusion.fresh_ref
  12.2 0.0 copy-done
  12.2 264.6 %shard_map.82 = bf16[256,2048]{1,0:T(8,128)(2,1)} custom-call(bf16[256,2048]{1,0:T(8,128)(2,1)} %q_ref.1, bf16[2048,256]{1,0:T(8,128)(2,1)} %k_ref.1, bf16[2048,256]{1,0:T(8,128)(2,1)} %v_ref.1, bf16[2,256,256]{2,1,0:T(8,128)(2,1)} %pad_maximum_fusion.fresh_ref, s32[24,256]{1,0:T(8,128)} %pad_add_fusion.meta_ref, s32[256,1]{1,0:T(8,128)} %copy.10.column_ref, ...), custom_call_target="tpu_custom_call" | custom-call | tf_op jit(solution)/shard_map/pallas_call | solution.py:301
  276.9 16.7 %convolution_convert_fusion = bf16[256,8192]{1,0:T(8,128)(2,1)} fusion(bf16[256,2048]{1,0:T(8,128)(2,1)} %shard_map.82, bf16[2048,8192]{1,0:T(8,128)(2,1)} %param.15), kind=kOutput, calls=%fused_computation | convolution fusion | flops 8592031744 | bytes 38797312 | tf_op jit(solution)/shard_map/dot_general | solution.py:366
  293.6 0.0 reduce-scatter.2.cloned.1.call-update
  293.6 42.9 %reduce-scatter.2.cloned.1.call-done = bf16[64,8192]{1,0:T(8,128)(2,1)} async-done(((bf16[256,8192]{1,0:T(8,128)(2,1)}), bf16[64,8192]{1,0:T(8,128)(2,1)}) %reduce-scatter.2.cloned.1.call-update) | async-done | bytes 1048592 | tf_op jit(solution)/shard_map/reduce_scatter | solution.py:367
  (3 shorter events, 0.0 us)
Async XLA Ops:
  6.5 330.0 %reduce-scatter.2.cloned.1.call-start = ((), (), s32[]{:S(2)}) async-start(), calls=%async_computation.1 | async-start | bytes 5242880 | tf_op jit(solution)/shard_map/reduce_scatter | solution.py:367
  7.6 4.6 %copy-start = (s32[16]{0:T(128)}, s32[16]{0:T(128)S(1)}, u32[]{:S(2)}) copy-start(s32[16]{0:T(128)S(1)} %get-tuple-element.6.slot_ref) | copy-start | bytes 196
Sparse Core Ops, SparseCore 0:
  293.7 42.7 reduce-scatter.1

commit v2 on v1

--- a/solution.py
+++ b/solution.py
@@ -26,9 +26,13 @@
 def attention_kernel(
     n, q_ref, k_ref, v_ref, fresh_ref, meta_ref, column_ref, slot_ref, out_ref,
     q_all, meta_all, fr_all, kk, vv, fk, fv, bias, qsel, o_out, o_in, l_out, l_in, fo, fl,
-    local_sem, kv_send, kv_recv, q_send, q_recv, m_send, m_recv, f_send, f_recv,
-    mp_send, fp_send, o_send, o_recv, l_send, l_recv,
+    *rest,
 ):
+    (local_sem, kv_send, kv_recv, q_send, q_recv, m_send, m_recv, f_send, f_recv,
+     mp_send, fp_send, o_send, o_recv, l_send, l_recv) = rest[-15:]
+    held_a, held_b, fheld_a, fheld_b = (rest[0], rest[1], rest[0], rest[1])
+    if n * q_ref.shape[0] != k_ref.shape[0]:
+        fheld_a, fheld_b = rest[2], rest[3]
     planes = n // 2
     tokens = q_ref.shape[0]
     heads = q_ref.shape[1] // HD
@@ -126,10 +130,6 @@
     for c in locals_[3:]:
         c.wait()
 
-    def soft(scores):
-        top = jnp.max(scores, axis=1, keepdims=True)
-        return top, jnp.exp2(scores - top).astype(jnp.bfloat16)
-
     def choose(s, e):
         g = 2 * s + par
         for r in range(CAP):
@@ -150,16 +150,21 @@
     def work(s, e, outs, logs):
         choose(s, e)
         span = 2 * block
-
-        def step(i, carry):
+        steps = heads // 2
+
+        def score(i, held):
             g = lax.div(i, per_group // 2)
-            q = qsel[pl.ds(2 * i, 2)].reshape(2 * span, HD)
-            scores = nt_dot(q, kk[e, g]) * SCALE2
-            top, weights = soft(scores)
+            scores = nt_dot(qsel[pl.ds(2 * i, 2)].reshape(2 * span, HD), kk[e, g])
+            held[...] = scores
+            return jnp.max(scores, axis=1, keepdims=True)
+
+        def finish(i, held, top):
+            g = lax.div(i, per_group // 2)
+            weights = jnp.exp2((held[...] - top) * SCALE2).astype(jnp.bfloat16)
             both = jnp.dot(weights, vv[e, g], preferred_element_type=jnp.float32)
             total = both[:, HD:]
             result = both[:, :HD] / total
-            log = top + jnp.log2(total)
+            log = top * SCALE2 + jnp.log2(total)
             for j in range(2):
                 h = 2 * i + j
                 lanes = pl.ds(pl.multiple_of(h * HD, HD), HD)
@@ -167,9 +172,15 @@
                     a = j * span + r * block
                     outs[s, e, r, :, lanes] = result[a:a + block].astype(jnp.bfloat16)
                     logs[s, e, r, pl.ds(h, 1), pl.ds(0, block)] = log[a:a + block].T[:1]
-            return carry
-
-        lax.fori_loop(0, heads // 2, step, 0)
+
+        def step(j, top):
+            later = score(2 * j + 1, held_b)
+            finish(2 * j, held_a, top)
+            top = score(jnp.minimum(2 * j + 2, steps - 1), held_a)
+            finish(2 * j + 1, held_b, later)
+            return top
+
+        lax.fori_loop(0, steps // 2, step, score(0, held_a))
 
     def returns(s, e):
         return (
@@ -177,15 +188,16 @@
             remote(l_out.at[s, e], l_in.at[here, e], l_send.at[s, e], l_recv.at[here, e], column(s)),
         )
 
-    def others(act):
+    def others(*acts):
         def at_distance(k, carry):
-            @pl.when(here - k >= 0)
-            def _():
-                act(here - k)
-
-            @pl.when(here + k < planes)
-            def _():
-                act(here + k)
+            for act in acts:
+                @pl.when(here - k >= 0)
+                def _():
+                    act(here - k)
+
+                @pl.when(here + k < planes)
+                def _():
+                    act(here + k)
 
             return carry
 
@@ -193,17 +205,19 @@
 
     work(here, par, o_in, l_in)
 
-    def first_half(s):
+    def pass_on(s):
         for kind in ("m", "q", "f"):
             chain(kind, s, None).wait_recv()
             on_sides(s, lambda side, kind=kind: chain(kind, s, side).start())
             if kind != "q":
                 to_mate(kind, s).start()
+
+    def first_half(s):
         work(s, par, o_out, l_out)
         for c in returns(s, par):
             c.start()
 
-    others(first_half)
+    others(pass_on, first_half)
     for c in kv_copies:
         c.wait()
 
@@ -233,18 +247,30 @@
     for g in range(groups):
         fv[g, :, HD:] = jnp.ones((n * tokens, HD), jnp.bfloat16)
 
-    def fresh_head(h, carry):
+    def fresh_score(h, held):
         g = lax.div(h, per_group)
         lanes = pl.ds(pl.multiple_of(h * HD, HD), HD)
-        scores = nt_dot(q_ref[:, lanes], fk[g]) * SCALE2 + bias[...]
-        top, weights = soft(scores)
+        scores = nt_dot(q_ref[:, lanes], fk[g]) + bias[...]
+        held[...] = scores
+        return jnp.max(scores, axis=1, keepdims=True)
+
+    def fresh_finish(h, held, top):
+        g = lax.div(h, per_group)
+        lanes = pl.ds(pl.multiple_of(h * HD, HD), HD)
+        weights = jnp.exp2((held[...] - top) * SCALE2).astype(jnp.bfloat16)
         both = jnp.dot(weights, fv[g], preferred_element_type=jnp.float32)
         total = both[:, HD:]
         fo[:, lanes] = both[:, :HD] / total
-        fl[h] = top + jnp.log2(total)
-        return carry
-
-    lax.fori_loop(0, heads, fresh_head, 0)
+        fl[h] = top * SCALE2 + jnp.log2(total)
+
+    def fresh_step(j, top):
+        later = fresh_score(2 * j + 1, fheld_b)
+        fresh_finish(2 * j, fheld_a, top)
+        top = fresh_score(jnp.minimum(2 * j + 2, heads - 1), fheld_a)
+        fresh_finish(2 * j + 1, fheld_b, later)
+        return top
+
+    lax.fori_loop(0, heads // 2, fresh_step, fresh_score(0, fheld_a))
 
     def arrived(s):
         for e in range(2):
@@ -298,6 +324,9 @@
     vmem = pl.BlockSpec(memory_space=pltpu.VMEM)
     bf, f32 = jnp.bfloat16, jnp.float32
     dma = pltpu.SemaphoreType.DMA
+    held = [pltpu.VMEM((tokens, span), f32)] * 2
+    if n * tokens != span:
+        held += [pltpu.VMEM((tokens, n * tokens), f32)] * 2
     return pl.pallas_call(
         functools.partial(attention_kernel, n),
         out_shape=jax.ShapeDtypeStruct((tokens, width), bf),
@@ -319,6 +348,7 @@
             pltpu.VMEM((planes, 2, CAP, heads, HD), f32),
             pltpu.VMEM((tokens, width), f32),
             pltpu.VMEM((heads, tokens, HD), f32),
+            *held,
             dma((3 + 2 * groups,)),
             dma((2 * groups,)),
             dma((2 * groups,)),
@@ -339,6 +369,137 @@
             collective_id=0, has_side_effects=True, vmem_limit_bytes=62 * 1024 * 1024
         ),
     )(queries, keys, values, fresh, meta, column, slots)
+
+
+def project_kernel(nt, a_ref, w_ref, out_ref, a2, wbuf, part, own, mate_out, mate_in, x_out, x_in,
+                   w_sem, mate_send, mate_recv, x_send, x_recv):
+    pairs = nt // 2
+    rows = a_ref.shape[0] // nt
+    count, wide = own.shape[0], own.shape[2]
+    me = lax.axis_index("tp")
+    core = lax.rem(me, 2)
+    x = lax.div(me, 2)
+    mate = {"tp": me + 1 - 2 * core}
+
+    def peer(d):
+        return lax.rem(x + d, pairs)
+
+    def fetch(j):
+        return pltpu.make_async_copy(
+            w_ref.at[:, pl.ds(pl.multiple_of(j * wide, wide), wide)],
+            wbuf.at[lax.rem(j, 2)], w_sem.at[lax.rem(j, 2)],
+        )
+
+    fetch(0).start()
+    fetch(1).start()
+    barrier = pltpu.get_barrier_semaphore()
+    for target in [mate] + [{"tp": 2 * peer(d) + core} for d in range(1, pairs)]:
+        pl.semaphore_signal(
+            barrier, inc=1, device_id=target, device_id_type=pl.DeviceIdType.MESH
+        )
+    pl.semaphore_wait(barrier, pairs)
+    for t in range(nt):
+        at = (t % 2) * pairs * rows + (t // 2) * rows
+        a2[at:at + rows, :] = a_ref[t * rows:(t + 1) * rows, :]
+
+    def swap(j):
+        return pltpu.make_async_remote_copy(
+            src_ref=mate_out.at[j], dst_ref=mate_in.at[j], send_sem=mate_send.at[j],
+            recv_sem=mate_recv.at[j], device_id=mate, device_id_type=pl.DeviceIdType.MESH,
+        )
+
+    def across(j, d):
+        return pltpu.make_async_remote_copy(
+            src_ref=x_out.at[j, peer(d)], dst_ref=x_in.at[j, x], send_sem=x_send.at[j, d],
+            recv_sem=x_recv.at[j, x], device_id={"tp": 2 * peer(d) + core},
+            device_id_type=pl.DeviceIdType.MESH,
+        )
+
+    def arrival(j, d):
+        return pltpu.make_async_remote_copy(
+            src_ref=x_out.at[j, peer(d)], dst_ref=x_in.at[j, peer(d)], send_sem=x_send.at[j, d],
+            recv_sem=x_recv.at[j, peer(d)], device_id={"tp": 2 * peer(d) + core},
+            device_id_type=pl.DeviceIdType.MESH,
+        )
+
+    def add_mate(j):
+        swap(j).wait_recv()
+        total = own[j] + mate_in[j].astype(jnp.float32)
+        own[j] = total
+        for k in range(pairs):
+            x_out[j, k] = total[k * rows:(k + 1) * rows].astype(jnp.bfloat16)
+        for d in range(1, pairs):
+            across(j, d).start()
+
+    def step(j, carry):
+        fetch(j).wait()
+        part[...] = jnp.dot(
+            a2[...], wbuf[lax.rem(j, 2)], preferred_element_type=jnp.float32
+        ).reshape(part.shape)
+        mate_out[j] = part[1 - core].astype(jnp.bfloat16)
+        swap(j).start()
+        own[j] = part[core]
+
+        @pl.when(j + 2 < count)
+        def _():
+            fetch(j + 2).start()
+
+        @pl.when(j >= 1)
+        def _():
+            add_mate(j - 1)
+
+        return carry
+
+    lax.fori_loop(0, count, step, 0)
+    add_mate(count - 1)
+
+    def last(j, carry):
+        total = own[j, pl.ds(pl.multiple_of(x * rows, rows), rows), :]
+        for d in range(1, pairs):
+            arrival(j, d).wait_recv()
+            total = total + x_in[j, peer(d)].astype(jnp.float32)
+        out_ref[:, pl.ds(pl.multiple_of(j * wide, wide), wide)] = total.astype(out_ref.dtype)
+        swap(j).wait_send()
+        for d in range(1, pairs):
+            across(j, d).wait_send()
+        return carry
+
+    lax.fori_loop(0, count, last, 0)
+
+
+def project(nt, attention, out_weight):
+    tokens, width = attention.shape
+    columns = out_weight.shape[1]
+    wide = 1024
+    count = columns // wide
+    pairs = nt // 2
+    rows = tokens // nt
+    bf, f32 = jnp.bfloat16, jnp.float32
+    dma = pltpu.SemaphoreType.DMA
+    return pl.pallas_call(
+        functools.partial(project_kernel, nt),
+        out_shape=jax.ShapeDtypeStruct((rows, columns), bf),
+        in_specs=[pl.BlockSpec(memory_space=pltpu.VMEM), pl.BlockSpec(memory_space=pl.ANY)],
+        out_specs=pl.BlockSpec(memory_space=pltpu.VMEM),
+        scratch_shapes=[
+            pltpu.VMEM((tokens, width), bf),
+            pltpu.VMEM((2, width, wide), bf),
+            pltpu.VMEM((2, tokens // 2, wide), f32),
+            pltpu.VMEM((count, tokens // 2, wide), f32),
+            pltpu.VMEM((count, tokens // 2, wide), bf),
+            pltpu.VMEM((count, tokens // 2, wide), bf),
+            pltpu.VMEM((count, pairs, rows, wide), bf),
+            pltpu.VMEM((count, pairs, rows, wide), bf),
+            dma((2,)),
+            dma((count,)),
+            dma((count,)),
+            dma((count, pairs)),
+            dma((count, pairs)),
+        ],
+        compiler_params=pltpu.CompilerParams(
+            collective_id=1, has_side_effects=True, vmem_limit_bytes=48 * 1024 * 1024
+        ),
+    )(attention, out_weight)
 
 
 def per_device(
@@ -363,8 +524,7 @@
     attention = attend(
         n, queries, cache_keys, cache_values, fresh, meta, positions.reshape(tokens, 1), slots
     )
-    part = jnp.dot(attention, out_weight, preferred_element_type=jnp.float32).astype(jnp.bfloat16)
-    return lax.psum_scatter(part, "tp", scatter_dimension=0, tiled=True)
+    return project(lax.axis_size("tp"), attention, out_weight)
 
 
 def solution(mesh):

time: 344 us -> 227 us (0.66)
  Pallas kernels: 265 us -> 218 us
  waiting for transfers between devices: 42.9 us -> 0 us
  matrix products: 16.7 us -> 0 us
  between operations: 13.4 us -> 0.04 us
    pallas_call x1, Pallas kernels: 265 us -> 188 us  [attend(): pl.pallas_call(functools.partial(attention_kernel, n), out_shape=jax.Shap...]
    reduce_scatter x1 -> x0, waiting for transfers between devices: 42.9 us -> none  [per_device(): return lax.psum_scatter(part, 'tp', scatter_dimension=0, tiled=True)]
    pallas_call x0 -> x1, Pallas kernels: none -> 30.4 us  [project(): pl.pallas_call(functools.partial(project_kernel, nt), out_shape=jax.Shape...]
    dot_general x1 -> x0, matrix products: 16.7 us -> none  [per_device(): jnp.dot(attention, out_weight, preferred_element_type=jnp.float32)]
  transfers between devices with their start and end apart: 1 -> 0, of which waited for: 1 -> 0; matrix products, arithmetic and copies ran while one was open for 0% -> 0% of each run, Pallas kernels for 0% -> 0%
where the time goes in v2:
time: 227 us; the launch traced here: 226 us
  Pallas kernels  218 us (96%)
  local copies, waits for them, and re-layouts  5.11 us (2%)
  other arithmetic  2.78 us (1%)
    pallas_call x1, Pallas kernels, attend(): pl.pallas_call(functools.partial(attention_kernel, n), out_shape=jax.Shap...  188 us
    pallas_call x1, Pallas kernels, project(): pl.pallas_call(functools.partial(project_kernel, nt), out_shape=jax.Shape...  30.4 us

profile of v2, /device:TPU:0, one launch (start us, length us, event | category | flops | bytes accessed | tf_op | source)
XLA Modules:
  0.0 226.4 jit_solution(10803971605724079932)
XLA Ops:
  0.0 0.8 reshape.30
  0.8 0.1 fusion
  0.9 0.2 select_reduce_fusion.1
  1.1 0.0 copy-start.1
  1.1 0.1 select_reduce_fusion
  1.2 0.7 broadcast_in_dim.5
  1.9 0.7 pad_add_fusion.meta_ref
  2.6 1.5 copy.10.column_ref
  4.0 1.7 pad_maximum_fusion.fresh_ref
  5.7 0.0 copy-done.1
  5.7 188.1 %shard_map.82.a_ref = bf16[256,2048]{1,0:T(8,128)(2,1)} custom-call(bf16[256,2048]{1,0:T(8,128)(2,1)} %q_ref.1, bf16[2048,256]{1,0:T(8,128)(2,1)} %k_ref.1, bf16[2048,256]{1,0:T(8,128)(2,1)} %v_ref.1, bf16[2,256,256]{2,1,0:T(8,128)(2,1)} %pad_maximum_fusion.fresh_ref, s32[24,256]{1,0:T(8,128)} %pad_add_fusion.meta_ref, s32[256,1]{1,0:T(8,128)} %copy.10.column_ref, ...), custom_call_target="tpu_custom_call" | custom-call | tf_op jit(solution)/shard_map/pallas_call | solution.py:330
  193.8 0.0 copy-start
  193.8 1.2 copy-done
  195.0 30.4 %shard_map.83 = bf16[64,8192]{1,0:T(8,128)(2,1)S(1)} custom-call(bf16[256,2048]{1,0:T(8,128)(2,1)S(1)} %copy-done, bf16[2048,8192]{1,0:T(8,128)(2,1)} %w_ref.1), custom_call_target="tpu_custom_call" | custom-call | tf_op jit(solution)/shard_map/pallas_call | solution.py:479
  225.5 1.0 copy.12
  (3 shorter events, 0.0 us)
Async XLA Ops:
  1.1 4.6 %copy-start.1 = (s32[16]{0:T(128)}, s32[16]{0:T(128)S(1)}, u32[]{:S(2)}) copy-start(s32[16]{0:T(128)S(1)} %get-tuple-element.6.slot_ref) | copy-start | bytes 196
  193.8 1.2 copy-start
